TPU v7x, 128 devices: a whole 4x4x4 slice. The times are simulated.
128 devices in a mesh: heads: 8 (over z_hi, x), ctx: 16 (over y, z_lo, core).
Axes of the slice: x: 4, y: 4, z: 4 (z_hi: 2, z_lo: 2; z = z_hi * 2 + z_lo), core: 2. Of those that a mesh axis runs over, the one named last changes fastest.
Arguments:
- queries: bfloat16 [16384, 8192], P('ctx', 'heads'), may hold values from -6 to 6
- keys: bfloat16 [16384, 1024], P('ctx', 'heads'), may hold values from -6 to 6
- values: bfloat16 [16384, 1024], P('ctx', 'heads'), may hold values from -6 to 6
- outputs: bfloat16 [16384, 8192], P('ctx', 'heads'), may hold values from -6 to 6
- out_grad: bfloat16 [16384, 5120], P('ctx', 'heads'), may hold values from -6 to 6
- out_weight: bfloat16 [8192, 5120], P('heads'), may hold values from -0.0625 to 0.0625
- log_norm: float32 [64, 16384], P('heads', 'ctx'), may hold values from 4 to 8
- doc_ids: int32 [16384], replicated, may hold values from 0 to 31, as said below
Outputs:
- grad_queries: bfloat16 [16384, 8192], P('ctx', 'heads')
- grad_keys: bfloat16 [16384, 1024], P('ctx', 'heads')
- grad_values: bfloat16 [16384, 1024], P('ctx', 'heads')
Inputs may be any that keep to these rules, and one draw needn't show every extreme that they name: `doc_ids`: document numbers never fall along the sequence; document 0 starts at token 0 and document k, for k of 1 or more, starts strictly inside the k-th half of a sequence block (tokens k * 512 + 1 onward, before (k + 1) * 512).
All inputs are finite; a program needn't handle non-finite values.
Results may differ from a plain program's by a relative error of at most 0.02.
Values may be sent and summed in bfloat16 or wider, within the bound.
A program may use at most 192 MiB of HBM per device.

v0:
```python
import math

import jax
import jax.numpy as jnp
from jax import lax
from jax.sharding import PartitionSpec as P

WIN_BLOCKS = 1


def from_behind(value, axis, steps):
    count = lax.axis_size(axis)
    first, last = (max(0, -steps), min(count, count - steps))
    return lax.ppermute(value, axis, [(source, source + steps) for source in range(first, last)])


def from_behind_2(block, axis, distance):
    devices = range(lax.axis_size(axis))
    route = [((i - distance) % len(devices), i) for i in devices]
    return lax.ppermute(block, axis, route)


def per_device(queries, keys, values, outputs, out_grad, out_weight, log_norm, doc_ids):
    tok_rows = keys.shape[0]
    head_dim = keys.shape[1]
    group = queries.shape[1] // head_dim
    half_rows = tok_rows // 2
    window = WIN_BLOCKS * tok_rows
    blocks = lax.axis_size("ctx")
    own_block = lax.axis_index("ctx")
    softmax_scale = 1.0 / math.sqrt(head_dim)
    grad_out = lax.dot_general(
        lax.all_gather(out_grad, "heads", axis=1, tiled=True),
        out_weight,
        (((1,), (1,)), ((), ())),
        preferred_element_type=jnp.float32,
    ).astype(jnp.bfloat16)
    products = grad_out.astype(jnp.float32) * outputs.astype(jnp.float32)
    delta_rows = jnp.sum(products.reshape(tok_rows, group, head_dim), axis=-1).T
    offsets = jnp.arange(half_rows, dtype=jnp.int32)

    def half_terms(
        query_part, grad_part, lse_part, delta_part, key_part, value_part, query_first, key_first
    ):
        query_ids = lax.dynamic_slice_in_dim(doc_ids, query_first, half_rows)
        key_ids = lax.dynamic_slice_in_dim(doc_ids, key_first, half_rows)
        query_pos = query_first + offsets
        key_pos = key_first + offsets
        allowed = (
            (query_ids[:, None] == key_ids[None, :])
            & (key_pos[None, :] <= query_pos[:, None])
            & (key_pos[None, :] > query_pos[:, None] - window)
        )
        query3 = query_part.reshape(half_rows, group, head_dim)
        grad3 = grad_part.reshape(half_rows, group, head_dim)
        scores = (
            jnp.einsum("qgd,kd->gqk", query3, key_part, preferred_element_type=jnp.float32)
            * softmax_scale
        )
        probs = jnp.where(allowed[None], jnp.exp(scores - lse_part[:, :, None]), 0.0)
        dprobs = jnp.einsum("qgd,kd->gqk", grad3, value_part, preferred_element_type=jnp.float32)
        dscores = probs * (dprobs - delta_part[:, :, None])
        probs_low = probs.astype(jnp.bfloat16)
        dscores_low = dscores.astype(jnp.bfloat16)
        value_term = jnp.einsum("gqk,qgd->kd", probs_low, grad3, preferred_element_type=jnp.float32)
        key_term = (
            jnp.einsum("gqk,qgd->kd", dscores_low, query3, preferred_element_type=jnp.float32)
            * softmax_scale
        )
        query_term = (
            jnp.einsum("gqk,kd->qgd", dscores_low, key_part, preferred_element_type=jnp.float32)
            * softmax_scale
        )
        return (query_term.reshape(half_rows, group * head_dim), key_term, value_term)

    def half_pair(
        query_part, grad_part, lse_part, delta_part, key_part, value_part, query_first, key_first
    ):
        return half_terms(
            query_part,
            grad_part,
            lse_part,
            delta_part,
            key_part,
            value_part,
            query_first,
            key_first,
        )

    def block_pair(
        query_blk, grad_blk, lse_blk, delta_blk, key_blk, value_blk, query_idx, key_idx, distance
    ):
        query_parts = []
        key_parts = [jnp.zeros((half_rows, head_dim), jnp.float32) for _ in range(2)]
        value_parts = [jnp.zeros((half_rows, head_dim), jnp.float32) for _ in range(2)]
        for query_half in range(2):
            query_sum = jnp.zeros((half_rows, group * head_dim), jnp.float32)
            rows = slice(query_half * half_rows, (query_half + 1) * half_rows)
            for key_half in range(2):
                query_low = distance * tok_rows + query_half * half_rows
                query_high = query_low + half_rows - 1
                key_low = key_half * half_rows
                key_high = key_low + half_rows - 1
                if query_high < key_low or query_low - key_high >= window:
                    continue
                cols = slice(key_half * half_rows, (key_half + 1) * half_rows)
                query_term, key_term, value_term = half_pair(
                    query_blk[rows],
                    grad_blk[rows],
                    lse_blk[:, rows],
                    delta_blk[:, rows],
                    key_blk[cols],
                    value_blk[cols],
                    query_idx * tok_rows + query_half * half_rows,
                    key_idx * tok_rows + key_half * half_rows,
                )
                query_sum = query_sum + query_term
                key_parts[key_half] = key_parts[key_half] + key_term
                value_parts[key_half] = value_parts[key_half] + value_term
            query_parts.append(query_sum)
        return (
            jnp.concatenate(query_parts, axis=0),
            jnp.concatenate(key_parts, axis=0),
            jnp.concatenate(value_parts, axis=0),
        )

    query_acc, key_acc, value_acc = block_pair(
        queries, grad_out, log_norm, delta_rows, keys, values, own_block, own_block, 0
    )
    query_blk, grad_blk, lse_blk, delta_blk = (queries, grad_out, log_norm, delta_rows)
    distance = 1
    query_blk, grad_blk = from_behind((query_blk, grad_blk), "ctx", -1)
    query_acc, lse_blk, delta_blk = from_behind_2((query_acc, lse_blk, delta_blk), "ctx", -1)
    anchor = (own_block + distance) % blocks
    query_term, key_term, value_term = block_pair(
        query_blk, grad_blk, lse_blk, delta_blk, keys, values, anchor, own_block, distance
    )
    query_acc = query_acc + query_term
    key_acc = key_acc + key_term
    value_acc = value_acc + value_term
    query_final = from_behind_2(query_acc.astype(jnp.bfloat16), "ctx", WIN_BLOCKS).astype(
        query_acc.dtype
    )
    return (
        query_final.astype(jnp.bfloat16),
        key_acc.astype(jnp.bfloat16),
        value_acc.astype(jnp.bfloat16),
    )


def solution(mesh):
    in_specs = (
        P("ctx", "heads"),
        P("ctx", "heads"),
        P("ctx", "heads"),
        P("ctx", "heads"),
        P("ctx", "heads"),
        P("heads", None),
        P("heads", "ctx"),
        P(),
    )
    out_specs = (P("ctx", "heads"), P("ctx", "heads"), P("ctx", "heads"))
    return jax.shard_map(
        per_device, mesh=mesh, in_specs=in_specs, out_specs=out_specs, check_vma=False
    )
```

profile of v0, /device:TPU:0, one launch (start us, length us, event | category | flops | bytes accessed | tf_op | source)
XLA Modules:
  0.0 324.8 jit_solution(2263753189306937314)
XLA Ops:
  7.9 4.0 %collective-permute-start.2 = (f32[8,1024]{1,0:T(8,128)}, f32[8,1024]{1,0:T(8,128)S(1)}, u32[]{:S(2)}, u32[]{:S(2)}) collective-permute-start(f32[8,1024]{1,0:T(8,128)} %param.14), channel_id=1, source_target_pairs={{1,0},{2,1},{3,2},{4,3},{5,4},{6,5},{7,6},{8,7},{9,8},{10,9},{11,1... | collective-permute-start | bytes 98312 | tf_op jit(solution)/shard_map/ppermute | solution.py:20
  11.9 3.9 %copy.46 = bf16[1024,1024]{0,1:T(8,128)(2,1)} copy(bf16[1024,1024]{1,0:T(8,128)(2,1)} %param.8) | data formatting | bytes 4194304 | tf_op args[0]
  18.9 4.9 %fusion.91 = f32[512,512,8]{1,0,2:T(8,128)} fusion(bf16[512,8,128]{0,2,1:T(8,128)(2,1)S(1)} %bitcast.265, bf16[1024,128]{1,0:T(8,128)(2,1)S(1)} %copy-done.6), kind=kOutput, calls=%fused_computation.104 | convolution fusion | flops 536870912 | bytes 9568256 | tf_op jit(solution)/shard_map/qgd,kd->gqk/dot_general | solution.py:57
  24.6 4.5 %fusion.103 = f32[512,512,8]{1,0,2:T(8,128)} fusion(bf16[512,8,128]{0,2,1:T(8,128)(2,1)S(1)} %bitcast.266, bf16[1024,128]{1,0:T(8,128)(2,1)S(1)} %copy-done.6), kind=kOutput, calls=%fused_computation.116 | convolution fusion | flops 536870912 | bytes 9568256 | tf_op jit(solution)/shard_map/qgd,kd->gqk/dot_general | solution.py:57
  29.0 4.5 %fusion.105 = f32[512,512,8]{1,0,2:T(8,128)} fusion(bf16[512,8,128]{0,2,1:T(8,128)(2,1)S(1)} %bitcast.275, bf16[1024,128]{1,0:T(8,128)(2,1)S(1)} %copy-done.6), kind=kOutput, calls=%fused_computation.118 | convolution fusion | flops 536870912 | bytes 9568256 | tf_op jit(solution)/shard_map/qgd,kd->gqk/dot_general | solution.py:57
  33.5 3.2 compare_and_fusion.1
  36.7 3.9 %copy.50 = bf16[1024,1024]{0,1:T(8,128)(2,1)} copy(bf16[1024,1024]{1,0:T(8,128)(2,1)} %param.11) | data formatting | bytes 4194304 | tf_op args[3]
  42.4 4.5 %fusion.89 = f32[512,512,8]{1,0,2:T(8,128)} fusion(bf16[512,8,128]{0,2,1:T(8,128)(2,1)S(1)} %bitcast.269, bf16[1024,128]{1,0:T(8,128)(2,1)S(1)} %copy-done.6), kind=kOutput, calls=%fused_computation.102 | convolution fusion | flops 536870912 | bytes 9568256 | tf_op jit(solution)/shard_map/qgd,kd->gqk/dot_general | solution.py:57
  46.9 4.6 %fusion.101 = f32[512,512,8]{1,0,2:T(8,128)} fusion(bf16[512,8,128]{0,2,1:T(8,128)(2,1)S(1)} %bitcast.270, bf16[1024,128]{1,0:T(8,128)(2,1)S(1)} %copy-done.6), kind=kOutput, calls=%fused_computation.114 | convolution fusion | flops 536870912 | bytes 9568256 | tf_op jit(solution)/shard_map/qgd,kd->gqk/dot_general | solution.py:57
  51.5 4.5 %fusion.87 = f32[512,512,8]{1,0,2:T(8,128)} fusion(bf16[512,8,128]{0,2,1:T(8,128)(2,1)S(1)} %bitcast.273, bf16[1024,128]{1,0:T(8,128)(2,1)S(1)} %copy-done.6), kind=kOutput, calls=%fused_computation.100 | convolution fusion | flops 536870912 | bytes 9568256 | tf_op jit(solution)/shard_map/qgd,kd->gqk/dot_general | solution.py:57
  56.0 100.5 %all-gather.2.cloned.1.call-done = bf16[1024,5120]{1,0:T(8,128)(2,1)} async-done(((bf16[1024,640]{1,0:T(8,128)(2,1)}), bf16[1024,5120]{1,0:T(8,128)(2,1)}) %all-gather.2.cloned.1.call-update) | async-done | bytes 10485776 | tf_op jit(solution)/shard_map/all_gather | solution.py:33
  156.5 18.1 %bitcast_reduce_fusion = (f32[1024,8]{0,1:T(8,128)S(1)}, bf16[1024,1024]{0,1:T(8,128)(2,1)}) fusion(bf16[1024,1024]{0,1:T(8,128)(2,1)} %copy.50, bf16[1024,5120]{1,0:T(8,128)(2,1)} %all-gather.2.cloned.1.call-done, bf16[1024,5120]{1,0:T(8,128)(2,1)} %param.13), kind=kOutput, calls=%fused_computation.45 | convolution fusion | flops 10742652928 | bytes 25198592 | tf_op jit(solution)/shard_map/dot_general | solution.py:32
  179.8 5.2 %fusion.17 = bf16[8,512,512]{1,2,0:T(8,128)(2,1)S(1)} fusion(f32[512,512,8]{1,0,2:T(8,128)} %fusion.103, f32[8,512]{1,0:T(8,128)S(1)} %get-tuple-element.22, f32[8,512]{1,0:T(8,128)S(1)} %get-tuple-element.20, pred[512,512]{0,1:T(8,128)(4,1)S(1)} %copy-done.26, bf16[512,8,128]{0,2,1:T(8,128)(2,1)S(1)} %bitcast.299, bf16[1024,128]{1,0:T(8,128)(2,1)S(1)} %copy-done.32), kind=kOutput, calls=%fused_computation.26 | convolution fusion | flops 549453824 | bytes 14057472 | tf_op jit(solution)/shard_map/qgd,kd->gqk/dot_general | solution.py:61
  201.4 4.5 %fusion.76 = f32[512,128]{1,0:T(8,128)} fusion(f32[512,128]{1,0:T(8,128)} %convolution_bitcast_fusion.4, bf16[8,512,512]{1,2,0:T(8,128)(2,1)} %copy-done.4, bf16[512,8,128]{0,2,1:T(8,128)(2,1)} %bitcast.276), kind=kOutput, calls=%fused_computation.81 | convolution fusion | flops 537001984 | bytes 5767168 | tf_op jit(solution)/shard_map/gqk,qgd->kd/dot_general | solution.py:67
  205.8 6.6 %fusion.13 = bf16[8,512,512]{1,2,0:T(8,128)(2,1)S(1)} fusion(f32[512,512,8]{1,0,2:T(8,128)} %fusion.91, f32[8,512]{1,0:T(8,128)S(1)} %get-tuple-element.22, f32[8,512]{1,0:T(8,128)S(1)} %get-tuple-element.20, pred[512,512]{0,1:T(8,128)(4,1)} %get-tuple-element.26, bf16[512,8,128]{0,2,1:T(8,128)(2,1)} %bitcast.300, bf16[1024,128]{1,0:T(8,128)(2,1)} %param.10), kind=kOutput, calls=%fused_computation.20 | convolution fusion | flops 549453824 | bytes 14057472 | tf_op jit(solution)/shard_map/qgd,kd->gqk/dot_general | solution.py:61
  219.9 4.3 %fusion.49 = f32[512,128]{1,0:T(8,128)} fusion(bf16[8,512,512]{1,2,0:T(8,128)(2,1)} %copy-done.5, bf16[512,8,128]{0,2,1:T(8,128)(2,1)S(1)} %bitcast.268), kind=kOutput, calls=%fused_computation.70 | convolution fusion | flops 536936448 | bytes 5505024 | tf_op jit(solution)/shard_map/gqk,qgd->kd/dot_general | solution.py:67
  224.2 6.0 %fusion.57 = f32[512,128]{1,0:T(8,128)} fusion(bf16[512,8,128]{0,2,1:T(8,128)(2,1)} %bitcast.301, f32[512,512,8]{1,0,2:T(8,128)} %fusion.91, f32[8,512]{1,0:T(8,128)S(1)} %get-tuple-element.20, pred[512,512]{0,1:T(8,128)(4,1)} %get-tuple-element.26), kind=kOutput, calls=%fused_computation.74 | convolution fusion | flops 545259520 | bytes 9977856 | tf_op jit(solution)/shard_map/gqk,qgd->kd/dot_general | solution.py:65
  235.3 3.4 %collective-permute-start = (f32[1024,1024]{1,0:T(8,128)}, f32[1024,1024]{1,0:T(8,128)}, u32[]{:S(2)}, u32[]{:S(2)}) collective-permute-start(f32[1024,1024]{1,0:T(8,128)} %pad_maximum_fusion), channel_id=1, source_target_pairs={{1,0},{2,1},{3,2},{4,3},{5,4},{6,5},{7,6},{8,7},{9,8},{10,9},{11,1... | collective-permute-start | bytes 12582920 | tf_op jit(solution)/shard_map/ppermute | solution.py:20
  250.2 5.0 %fusion.9 = bf16[8,512,512]{1,2,0:T(8,128)(2,1)S(1)} fusion(f32[512,512,8]{1,0,2:T(8,128)} %fusion.101, f32[8,512]{1,0:T(8,128)S(1)} %get-tuple-element.17, f32[8,512]{1,0:T(8,128)S(1)} %get-tuple-element.15, pred[512,512]{0,1:T(8,128)(4,1)} %get-tuple-element.24, bf16[512,8,128]{0,2,1:T(8,128)(2,1)S(1)} %bitcast.293, bf16[1024,128]{1,0:T(8,128)(2,1)} %param.10), kind=kOutput, calls=%fused_computation.14 | convolution fusion | flops 549453824 | bytes 14057472 | tf_op jit(solution)/shard_map/qgd,kd->gqk/dot_general | solution.py:61
  256.0 5.5 %fusion.5 = bf16[8,512,512]{1,2,0:T(8,128)(2,1)S(1)} fusion(f32[512,512,8]{1,0,2:T(8,128)} %fusion.89, f32[8,512]{1,0:T(8,128)S(1)} %get-tuple-element.17, f32[8,512]{1,0:T(8,128)S(1)} %get-tuple-element.15, pred[512,512]{0,1:T(8,128)(4,1)S(1)} %copy-done.21, bf16[512,8,128]{0,2,1:T(8,128)(2,1)S(1)} %bitcast.294, bf16[1024,128]{1,0:T(8,128)(2,1)S(1)} %copy-done.34), kind=kOutput, calls=%fused_computation.8 | convolution fusion | flops 549453824 | bytes 14057472 | tf_op jit(solution)/shard_map/qgd,kd->gqk/dot_general | solution.py:61
  267.2 3.6 %convolution_bitcast_fusion = f32[512,128]{1,0:T(8,128)S(1)} fusion(bf16[8,512,512]{1,2,0:T(8,128)(2,1)} %copy-done, bf16[512,8,128]{0,2,1:T(8,128)(2,1)S(1)} %bitcast.274), kind=kOutput, calls=%fused_computation.64 | convolution fusion | flops 536870912 | bytes 5505024 | tf_op jit(solution)/shard_map/gqk,qgd->kd/dot_general | solution.py:67
  270.8 3.7 %fusion.50 = f32[512,128]{1,0:T(8,128)S(1)} fusion(bf16[8,512,512]{1,2,0:T(8,128)(2,1)} %copy-done.1, bf16[512,8,128]{0,2,1:T(8,128)(2,1)S(1)} %bitcast.271), kind=kOutput, calls=%fused_computation.71 | convolution fusion | flops 536936448 | bytes 5505024 | tf_op jit(solution)/shard_map/gqk,qgd->kd/dot_general | solution.py:67
  276.6 8.4 %collective-permute-done = f32[1024,1024]{1,0:T(8,128)} collective-permute-done((f32[1024,1024]{1,0:T(8,128)}, f32[1024,1024]{1,0:T(8,128)}, u32[]{:S(2)}, u32[]{:S(2)}) %collective-permute-start) | collective-permute-done | bytes 4194336 | tf_op jit(solution)/shard_map/ppermute | solution.py:20
  295.7 20.4 %collective-permute-done.5 = bf16[1024,1024]{1,0:T(8,128)(2,1)S(1)} collective-permute-done((bf16[1024,1024]{1,0:T(8,128)(2,1)S(1)}, bf16[1024,1024]{1,0:T(8,128)(2,1)S(1)}, u32[]{:S(2)}, u32[]{:S(2)}) %collective-permute-start.5) | collective-permute-done | bytes 2097184 | tf_op jit(solution)/shard_map/ppermute | solution.py:20
  (149 shorter events, 71.8 us)
Async XLA Ops:
  7.2 11.7 %copy-start.6 = (bf16[1024,128]{1,0:T(8,128)(2,1)S(1)}, bf16[1024,128]{1,0:T(8,128)(2,1)}, u32[]{:S(2)}) copy-start(bf16[1024,128]{1,0:T(8,128)(2,1)} %param.9) | copy-start | bytes 786436
  7.2 149.3 %all-gather.2.cloned.1.call-start = ((), (), s32[]{:S(2)}) async-start(), calls=%async_computation | async-start | bytes 11796480 | tf_op jit(solution)/shard_map/all_gather | solution.py:33
  7.9 32.8 %collective-permute-start.2 = (f32[8,1024]{1,0:T(8,128)}, f32[8,1024]{1,0:T(8,128)S(1)}, u32[]{:S(2)}, u32[]{:S(2)}) collective-permute-start(f32[8,1024]{1,0:T(8,128)} %param.14), channel_id=1, source_target_pairs={{1,0},{2,1},{3,2},{4,3},{5,4},{6,5},{7,6},{8,7},{9,8},{10,9},{11,1... | collective-permute-start | bytes 98312 | tf_op jit(solution)/shard_map/ppermute | solution.py:20
  15.8 24.9 %collective-permute-start.1 = (bf16[1024,1024]{0,1:T(8,128)(2,1)}, bf16[1024,1024]{0,1:T(8,128)(2,1)}, u32[]{:S(2)}, u32[]{:S(2)}) collective-permute-start(bf16[1024,1024]{0,1:T(8,128)(2,1)} %copy.46), channel_id=1, source_target_pairs={{1,0},{2,1},{3,2},{4,3},{5,4},{6,5},{7,6},{8,7},{9,8},{10,9},{11,1... | collective-permute-start | bytes 6291464 | tf_op jit(solution)/shard_map/ppermute | solution.py:14
  18.8 10.2 %copy-start.7 = (bf16[512,1024]{0,1:T(8,128)(2,1)}, bf16[512,1024]{0,1:T(8,128)(2,1)S(1)}, u32[]{:S(2)}) copy-start(bf16[512,1024]{0,1:T(8,128)(2,1)S(1)} %get-tuple-element.9) | copy-start | bytes 3145732
  24.6 12.2 %copy-start.31 = (f32[8,1024]{1,0:T(8,128)S(1)}, f32[8,1024]{1,0:T(8,128)}, u32[]{:S(2)}) copy-start(f32[8,1024]{1,0:T(8,128)} %param.14) | copy-start | bytes 98308
  156.5 23.3 %copy-start.26 = (pred[512,512]{0,1:T(8,128)(4,1)S(1)}, pred[512,512]{0,1:T(8,128)(4,1)}, u32[]{:S(2)}) copy-start(pred[512,512]{0,1:T(8,128)(4,1)} %get-tuple-element.25) | copy-start | bytes 786436
  156.5 23.3 %copy-start.32 = (bf16[1024,128]{1,0:T(8,128)(2,1)S(1)}, bf16[1024,128]{1,0:T(8,128)(2,1)}, u32[]{:S(2)}) copy-start(bf16[1024,128]{1,0:T(8,128)(2,1)} %param.10) | copy-start | bytes 786436
  174.6 64.0 %collective-permute-start.4 = (f32[8,1024]{1,0:T(8,128)S(1)}, f32[8,1024]{1,0:T(8,128)S(1)}, u32[]{:S(2)}, u32[]{:S(2)}) collective-permute-start(f32[8,1024]{1,0:T(8,128)S(1)} %bitcast.306), channel_id=1, source_target_pairs={{1,0},{2,1},{3,2},{4,3},{5,4},{6,5},{7,6},{8,7},{9,8},{10,9},{11,1... | collective-permute-start | bytes 98312 | tf_op jit(solution)/shard_map/ppermute | solution.py:20
  176.5 12.7 %slice-start.10 = ((s8[8388608]{0:T(1024)(128)(4,1)}), s8[4194304]{0:T(1024)(128)(4,1)S(1)}, s32[]{:S(2)}) async-start(s8[8388608]{0:T(1024)(128)(4,1)} %bitcast.289), calls=%async_computation.11 | async-start | bytes 8388608
  178.3 60.3 %collective-permute-start.3 = (bf16[1024,1024]{0,1:T(8,128)(2,1)}, bf16[1024,1024]{0,1:T(8,128)(2,1)}, u32[]{:S(2)}, u32[]{:S(2)}) collective-permute-start(bf16[1024,1024]{0,1:T(8,128)(2,1)} %get-tuple-element.30), channel_id=1, source_target_pairs={{1,0},{2,1},{3,2},{4,3},{5,4},{6,5},{7,6},{8,7},{9,8},{10,9},{11,1... | collective-permute-start | bytes 6291464 | tf_op jit(solution)/shard_map/ppermute | solution.py:14
  179.8 9.4 %slice-start.11 = ((s8[8388608]{0:T(1024)(128)(4,1)}), s8[4194304]{0:T(1024)(128)(4,1)S(1)}, s32[]{:S(2)}) async-start(s8[8388608]{0:T(1024)(128)(4,1)} %bitcast.289), calls=%async_computation.12 | async-start | bytes 8388608
  219.9 10.4 %slice-start.8 = ((s8[8388608]{0:T(1024)(128)(4,1)}), s8[4194304]{0:T(1024)(128)(4,1)S(1)}, s32[]{:S(2)}) async-start(s8[8388608]{0:T(1024)(128)(4,1)} %bitcast.287), calls=%async_computation.9 | async-start | bytes 8388608
  224.2 16.2 %slice-start.4 = ((s8[8388608]{0:T(1024)(128)(4,1)}), s8[4194304]{0:T(1024)(128)(4,1)S(1)}, s32[]{:S(2)}) async-start(s8[8388608]{0:T(1024)(128)(4,1)} %bitcast.283), calls=%async_computation.5 | async-start | bytes 8388608
  230.3 10.1 %slice-start.5 = ((s8[8388608]{0:T(1024)(128)(4,1)}), s8[4194304]{0:T(1024)(128)(4,1)S(1)}, s32[]{:S(2)}) async-start(s8[8388608]{0:T(1024)(128)(4,1)} %bitcast.283), calls=%async_computation.6 | async-start | bytes 8388608
  235.3 49.7 %collective-permute-start = (f32[1024,1024]{1,0:T(8,128)}, f32[1024,1024]{1,0:T(8,128)}, u32[]{:S(2)}, u32[]{:S(2)}) collective-permute-start(f32[1024,1024]{1,0:T(8,128)} %pad_maximum_fusion), channel_id=1, source_target_pairs={{1,0},{2,1},{3,2},{4,3},{5,4},{6,5},{7,6},{8,7},{9,8},{10,9},{11,1... | collective-permute-start | bytes 12582920 | tf_op jit(solution)/shard_map/ppermute | solution.py:20
  240.4 15.6 %copy-start.14 = (bf16[512,1024]{0,1:T(8,128)(2,1)}, bf16[512,1024]{0,1:T(8,128)(2,1)S(1)}, u32[]{:S(2)}) copy-start(bf16[512,1024]{0,1:T(8,128)(2,1)S(1)} %get-tuple-element.3) | copy-start | bytes 3145732
  267.2 17.8 %copy-start.8 = (f32[512,1024]{1,0:T(8,128)S(1)}, f32[512,1024]{1,0:T(8,128)}, u32[]{:S(2)}) copy-start(f32[512,1024]{1,0:T(8,128)} %copy.83) | copy-start | bytes 6291460
  267.2 17.8 %copy-start.9 = (f32[512,1024]{1,0:T(8,128)S(1)}, f32[512,1024]{1,0:T(8,128)}, u32[]{:S(2)}) copy-start(f32[512,1024]{1,0:T(8,128)} %copy.82) | copy-start | bytes 6291460
  274.5 14.0 %slice-start.6 = ((s8[8388608]{0:T(1024)(128)(4,1)}), s8[4194304]{0:T(1024)(128)(4,1)S(1)}, s32[]{:S(2)}) async-start(s8[8388608]{0:T(1024)(128)(4,1)} %bitcast.285), calls=%async_computation.7 | async-start | bytes 8388608
  274.5 14.0 %copy-start.17 = (bf16[512,1024]{0,1:T(8,128)(2,1)S(1)}, bf16[512,1024]{0,1:T(8,128)(2,1)}, u32[]{:S(2)}) copy-start(bf16[512,1024]{0,1:T(8,128)(2,1)} %copy-done.16) | copy-start | bytes 3145732
  274.5 14.0 %copy-start.25 = (pred[512,512]{0,1:T(8,128)(4,1)S(1)}, pred[512,512]{0,1:T(8,128)(4,1)}, u32[]{:S(2)}) copy-start(pred[512,512]{0,1:T(8,128)(4,1)} %get-tuple-element.28) | copy-start | bytes 786436
  276.6 11.9 %slice-start.7 = ((s8[8388608]{0:T(1024)(128)(4,1)}), s8[4194304]{0:T(1024)(128)(4,1)S(1)}, s32[]{:S(2)}) async-start(s8[8388608]{0:T(1024)(128)(4,1)} %bitcast.285), calls=%async_computation.8 | async-start | bytes 8388608
  288.1 28.1 %collective-permute-start.5 = (bf16[1024,1024]{1,0:T(8,128)(2,1)S(1)}, bf16[1024,1024]{1,0:T(8,128)(2,1)S(1)}, u32[]{:S(2)}, u32[]{:S(2)}) collective-permute-start(bf16[1024,1024]{1,0:T(8,128)(2,1)S(1)} %fusion.30), channel_id=1, source_target_pairs={{15,0},{0,1},{1,2},{2,3},{3,4},{4,5},{5,6},{6,7},{7,8},{8,9},{9,10... | collective-permute-start | bytes 6291464 | tf_op jit(solution)/shard_map/ppermute | solution.py:20
  (31 other events, 148.8 us)
Sparse Core Ops, SparseCore 0:
  10.3 146.0 all-gather.1
where the time goes:
time: 329 us; the launch traced here: 325 us
  waiting for transfers between devices  130 us (40%)
  matrix products  120 us (36%)
  local copies, waits for them, and re-layouts  36.5 us (11%)
  between operations  15.2 us (5%)
  starting transfers between devices  12.3 us (4%)
  other arithmetic  10.4 us (3%)
    all_gather x1, waiting for transfers between devices, per_device(): lax.all_gather(out_grad, 'heads', axis=1, tiled=True)  101 us
    ppermute x4, waiting for transfers between devices, from_behind_2(): return lax.ppermute(block, axis, route)  28.9 us
    dot_general x6, matrix products, half_terms(): jnp.einsum('qgd,kd->gqk', grad3, value_part, preferred_element_type=jnp.f...  28 us
    dot_general x6, matrix products, half_terms(): jnp.einsum('qgd,kd->gqk', query3, key_part, preferred_element_type=jnp.fl...  27.4 us
    dot_general x6, matrix products, half_terms(): jnp.einsum('gqk,qgd->kd', dscores_low, query3, preferred_element_type=jnp...  19.2 us
    dot_general x1, matrix products, per_device(): lax.dot_general(lax.all_gather(out_grad, 'heads', axis=1, tiled=True), ou...  18.1 us
    unnamed x99, local copies, waits for them, and re-layouts  17 us
    dot_general x6, matrix products, half_terms(): jnp.einsum('gqk,qgd->kd', probs_low, grad3, preferred_element_type=jnp.fl...  15.4 us
  transfers between devices with their start and end apart: 7, of which 3 were waited for; matrix products, arithmetic and copies ran while one was open for 42% of the time, Pallas kernels for 0%

commit v1 on v0

v1 whole, which is shorter than its diff:
```python
import functools
import math

import jax
import jax.numpy as jnp
from jax import lax
from jax.experimental import pallas as pl
from jax.experimental.pallas import tpu as pltpu
from jax.sharding import PartitionSpec as P

MESH = pl.DeviceIdType.MESH
TOK = 1024
HALF = 512
HD = 128
GROUP = 8
COLS = 640
D = 5120
QT = 256
ROWS = 64
CHUNKS = TOK // ROWS
PER_TILE = QT // ROWS
FLOWS = 8
LOG2E = math.log2(math.e)
NT = (((1,), (1,)), ((), ()))
NN = (((1,), (0,)), ((), ()))


def dot(a, b, dims):
    return lax.dot_general(a, b, dims, preferred_element_type=jnp.float32)


def kernel(
    q_hbm, k_hbm, v_hbm, o_hbm, og_hbm, w_hbm, lse_ref, doc_ref,
    dq_ref, dk_ref, dv_ref,
    gat, wv, qv, ov, ot, key, val, key_t, dk_acc, dv_acc, dk_in, dv_in, bias, doc_col, doc_row,
    send, recv, kv_send, kv_recv, back_send, back_recv, load,
):
    heads = lax.axis_index("heads")
    ctx = lax.axis_index("ctx")
    n_ctx = lax.axis_size("ctx")
    plane, x = heads // 4, heads % 4
    x_left, x_right, x_far = (x + 3) % 4, (x + 1) % 4, (x + 2) % 4
    other = 1 - plane
    right = {"heads": plane * 4 + x_right}
    left = {"heads": plane * 4 + x_left}
    across = {"heads": other * 4 + x}
    after = {"ctx": (ctx + 1) % n_ctx}
    before = {"ctx": (ctx + n_ctx - 1) % n_ctx}

    def cell(pl_, x_, row, rows):
        col = pl.multiple_of((pl_ * 4 + x_) * COLS, 128)
        return gat.at[pl.ds(row, rows), pl.ds(col, COLS)]

    def flow(f, j, received=False):
        r0 = pl.multiple_of(j * ROWS, ROWS)
        hr = ROWS // 2
        if f < 3:
            to = (right, left, across)[f]
            mine = cell(plane, x, r0, ROWS)
            src = og_hbm.at[pl.ds(r0, ROWS), :]
            got = (cell(plane, x_left, r0, ROWS), cell(plane, x_right, r0, ROWS), cell(other, x, r0, ROWS))[f]
        elif f == 3:
            to = right
            mine = src = cell(plane, x_left, r0, hr)
            got = cell(plane, x_far, r0, hr)
        elif f == 4:
            to = left
            mine = src = cell(plane, x_right, r0 + hr, hr)
            got = cell(plane, x_far, r0 + hr, hr)
        elif f in (5, 6):
            to = (right, left)[f - 5]
            mine = src = cell(other, x, r0, ROWS)
            got = cell(other, (x_left, x_right)[f - 5], r0, ROWS)
        else:
            to = across
            mine = src = cell(plane, x_far, r0, ROWS)
            got = cell(other, x_far, r0, ROWS)
        dst = mine
        if received:
            src = dst = got
        return pltpu.make_async_remote_copy(
            src_ref=src, dst_ref=dst, send_sem=send.at[f, j], recv_sem=recv.at[f, j],
            device_id=to, device_id_type=MESH,
        )

    def start(f, j):
        flow(f, j).start()

    def arrived(f, j):
        flow(f, j, received=True).wait_recv()

    def own(j):
        for f in range(3):
            start(f, j)

    def stage_a(j):
        arrived(0, j)
        start(3, j)
        arrived(1, j)
        start(4, j)
        arrived(2, j)
        start(5, j)
        start(6, j)

    def stage_b(j):
        arrived(3, j)
        arrived(4, j)
        start(7, j)

    def stage_c(j):
        for f in (5, 6, 7):
            arrived(f, j)

    def slot(t):
        @pl.when(t + 4 < CHUNKS)
        def _():
            own(t + 4)

        @pl.when(t + 2 < CHUNKS)
        def _():
            stage_a(t + 2)

        @pl.when(t + 1 < CHUNKS)
        def _():
            stage_b(t + 1)

        stage_c(t)

    def kv_copy(i, received=False):
        buf = (key, val)[i]
        src = (k_hbm, v_hbm)[i].at[pl.ds(HALF, HALF), :]
        dst = buf.at[pl.ds(0, HALF), :]
        return pltpu.make_async_remote_copy(
            src_ref=src, dst_ref=dst, send_sem=kv_send.at[i], recv_sem=kv_recv.at[i],
            device_id=after, device_id_type=MESH,
        )

    def back_copy(i):
        return pltpu.make_async_remote_copy(
            src_ref=(dk_acc, dv_acc)[i].at[pl.ds(0, HALF), :], dst_ref=(dk_in, dv_in)[i],
            send_sem=back_send.at[i], recv_sem=back_recv.at[i],
            device_id=before, device_id_type=MESH,
        )

    loads = [
        pltpu.make_async_copy(k_hbm, key.at[pl.ds(HALF, TOK), :], load.at[0]),
        pltpu.make_async_copy(v_hbm, val.at[pl.ds(HALF, TOK), :], load.at[1]),
        pltpu.make_async_copy(o_hbm, ov, load.at[2]),
        pltpu.make_async_copy(og_hbm, cell(plane, x, 0, TOK), load.at[3]),
        pltpu.make_async_copy(q_hbm, qv, load.at[4]),
        pltpu.make_async_copy(w_hbm, wv, load.at[5]),
    ]
    for c in loads:
        c.start()

    barrier = pltpu.get_barrier_semaphore()
    for d in (right, left, across, after, before):
        pl.semaphore_signal(barrier, inc=1, device_id=d, device_id_type=MESH)
    pl.semaphore_wait(barrier, 5)
    for j in range(4):
        own(j)
    for i in range(2):
        kv_copy(i).start()

    dk_acc[...] = jnp.zeros_like(dk_acc)
    dv_acc[...] = jnp.zeros_like(dv_acc)
    half = ctx * 2
    n_half = n_ctx * 2
    for b in range(3):
        docs = doc_ref[(half + n_half - 1 + b) % n_half].astype(jnp.float32)
        doc_row[:, b * HALF:(b + 1) * HALF] = docs
        doc_col[b * HALF:(b + 1) * HALF, :] = jnp.broadcast_to(docs, (128, HALF)).T

    loads[0].wait()
    loads[1].wait()
    key_t[:, HALF:] = key[HALF:, :].T
    loads[2].wait()

    def turn(h, carry):
        c0 = pl.multiple_of(h * HD, HD)
        ot[pl.ds(c0, HD), :] = ov[:, pl.ds(c0, HD)].T
        return carry

    stage_a(0)
    lax.fori_loop(0, GROUP, turn, 0)
    for c in loads[3:]:
        c.wait()
    stage_a(1)
    stage_b(0)
    for i in range(2):
        kv_copy(i).wait_recv()
    key_t[:, :HALF] = key[:HALF, :].T

    scale = 1.0 / math.sqrt(HD)

    def set_bias(i):
        k0, kk = (i // 2) * HALF, 768 + (i % 2) * QT
        q0 = HALF + i * QT
        row = doc_row[:, q0:q0 + QT]
        for part in range(kk // QT):
            lo = k0 + part * QT
            col = doc_col[lo:lo + QT, :]
            same = jnp.concatenate([col, col], axis=1) == row
            if lo == q0:
                kp = lax.broadcasted_iota(jnp.int32, (QT, QT), 0)
                qp = lax.broadcasted_iota(jnp.int32, (QT, QT), 1)
                same = same & (kp <= qp)
            bias[part * QT:(part + 1) * QT, :] = jnp.where(same, 0.0, -1e30)

    def piece(i, hp):
        k0, kk = (i // 2) * HALF, 768 + (i % 2) * QT
        r0 = i * QT
        f0 = pl.multiple_of(hp * 2 * HD, 2 * HD)
        got = dot(wv[pl.ds(f0, 2 * HD), :], gat[r0:r0 + QT, :], NT).astype(jnp.bfloat16)
        for a in range(2):
            h = hp * 2 + a
            c0 = pl.multiple_of(h * HD, HD)
            g = got[a * HD:(a + 1) * HD]
            q = qv[r0:r0 + QT, pl.ds(c0, HD)]
            o = ot[pl.ds(c0, HD), r0:r0 + QT]
            delta = jnp.sum(g.astype(jnp.float32) * o.astype(jnp.float32), axis=0, keepdims=True)
            lse = lse_ref[pl.ds(h, 1), r0:r0 + QT] * LOG2E
            kb = key[k0:k0 + kk, :]
            s = dot(kb, q, NT)
            p = jnp.exp2((s * (scale * LOG2E) - lse) + bias[:kk, :])
            dp = dot(val[k0:k0 + kk, :], g, NN)
            ds = (p * (dp - delta)).astype(jnp.bfloat16)
            dv_acc[k0:k0 + kk, :] += dot(p.astype(jnp.bfloat16), g, NT)
            dk_acc[k0:k0 + kk, :] += dot(ds, q, NN)
            dq_t = dot(key_t[:, k0:k0 + kk], ds, NN) * scale
            dq_ref[r0:r0 + QT, pl.ds(c0, HD)] = dq_t.T.astype(jnp.bfloat16)

    def step(t, carry):
        slot(t)
        return carry

    lax.fori_loop(0, PER_TILE, step, 0)
    for i in range(TOK // QT):
        set_bias(i)

        def body(hp, carry, i=i):
            if i + 1 < TOK // QT:
                slot((i + 1) * PER_TILE + hp)
            piece(i, hp)
            return carry

        lax.fori_loop(0, PER_TILE, body, 0)
        if i == 1:
            for b in range(2):
                back_copy(b).start()

    for b in range(2):
        back_copy(b).wait()
        kv_copy(b).wait_send()

    def drain(j, carry):
        for f in range(FLOWS):
            flow(f, j).wait_send()
        return carry

    lax.fori_loop(0, CHUNKS, drain, 0)
    dk_ref[:HALF, :] = (dk_acc[HALF:TOK, :] * scale).astype(jnp.bfloat16)
    dk_ref[HALF:, :] = ((dk_acc[TOK:, :] + dk_in[...]) * scale).astype(jnp.bfloat16)
    dv_ref[:HALF, :] = dv_acc[HALF:TOK, :].astype(jnp.bfloat16)
    dv_ref[HALF:, :] = (dv_acc[TOK:, :] + dv_in[...]).astype(jnp.bfloat16)


def per_device(queries, keys, values, outputs, out_grad, out_weight, log_norm, doc_ids):
    bf, f32 = jnp.bfloat16, jnp.float32
    any_ = pl.BlockSpec(memory_space=pl.ANY)
    vm = pl.BlockSpec(memory_space=pltpu.VMEM)
    dma = pltpu.SemaphoreType.DMA
    wide = HALF + TOK
    return pl.pallas_call(
        kernel,
        out_shape=(
            jax.ShapeDtypeStruct((TOK, GROUP * HD), bf),
            jax.ShapeDtypeStruct((TOK, HD), bf),
            jax.ShapeDtypeStruct((TOK, HD), bf),
        ),
        in_specs=[any_] * 6 + [vm] * 2,
        out_specs=(vm, vm, vm),
        scratch_shapes=[
            pltpu.VMEM((TOK, D), bf),
            pltpu.VMEM((GROUP * HD, D), bf),
            pltpu.VMEM((TOK, GROUP * HD), bf),
            pltpu.VMEM((TOK, GROUP * HD), bf),
            pltpu.VMEM((GROUP * HD, TOK), bf),
            pltpu.VMEM((wide, HD), bf),
            pltpu.VMEM((wide, HD), bf),
            pltpu.VMEM((HD, wide), bf),
            pltpu.VMEM((wide, HD), f32),
            pltpu.VMEM((wide, HD), f32),
            pltpu.VMEM((HALF, HD), f32),
            pltpu.VMEM((HALF, HD), f32),
            pltpu.VMEM((TOK, QT), f32),
            pltpu.VMEM((wide, 128), f32),
            pltpu.VMEM((1, wide), f32),
            dma((FLOWS, CHUNKS)),
            dma((FLOWS, CHUNKS)),
            dma((2,)), dma((2,)), dma((2,)), dma((2,)), dma((6,)),
        ],
        compiler_params=pltpu.CompilerParams(
            collective_id=0, has_side_effects=True, vmem_limit_bytes=58 * 2**20
        ),
        name="attention_backward",
    )(queries, keys, values, outputs, out_grad, out_weight, log_norm, doc_ids.reshape(32, 1, HALF))


def solution(mesh):
    in_specs = (
        P("ctx", "heads"), P("ctx", "heads"), P("ctx", "heads"), P("ctx", "heads"), P("ctx", "heads"),
        P("heads", None), P("heads", "ctx"), P(),
    )
    out_specs = (P("ctx", "heads"), P("ctx", "heads"), P("ctx", "heads"))
    return jax.shard_map(per_device, mesh=mesh, in_specs=in_specs, out_specs=out_specs, check_vma=False)
```

time: 329 us -> 120 us (0.36); the launches traced: 325 us -> 120 us
  waiting for transfers between devices: 130 us -> 0 us
  matrix products: 120 us -> 0 us
  Pallas kernels: 0 us -> 115 us
  local copies, waits for them, and re-layouts: 36.5 us -> 4.55 us
  between operations: 15.2 us -> 0.66 us
  starting transfers between devices: 12.3 us -> 0 us
  other arithmetic: 10.4 us -> 0 us
    dot_general x31 -> x0, matrix products: 120 us -> none  [the longest x6 28 us: half_terms(): jnp.einsum('qgd,kd->gqk', grad3, value_part, preferred_element_type=jnp.f...]
    pallas_call x0 -> x1, Pallas kernels: none -> 115 us  [per_device(): pl.pallas_call(kernel, out_shape=(jax.ShapeDtypeStruct((TOK, GROUP * HD),...]
    all_gather x1 -> x0, waiting for transfers between devices: 101 us -> none  [per_device(): lax.all_gather(out_grad, 'heads', axis=1, tiled=True)]
    ppermute x6 -> x0, waiting for transfers between devices: 28.9 us -> none  [the longest x4 28.9 us: from_behind_2(): return lax.ppermute(block, axis, route)]
    unnamed x99 -> x7, local copies, waits for them, and re-layouts: 17 us -> 4.55 us
    ppermute x6 -> x0, starting transfers between devices: 12.3 us -> none  [the longest x4 9.55 us: from_behind_2(): return lax.ppermute(block, axis, route)]
    slice x8 -> x0, local copies, waits for them, and re-layouts: 6.87 us -> none  [the longest x2 3.5 us: block_pair(): grad_blk[rows]]
    add x2 -> x0, local copies, waits for them, and re-layouts: 6.04 us -> none  [block_pair(): query_sum = query_sum + query_term]
  transfers between devices with their start and end apart: 7 -> 0, of which waited for: 3 -> 0; matrix products, arithmetic and copies ran while one was open for 42% -> 0% of each run, Pallas kernels for 0% -> 0%
where the time goes in v1:
time: 120 us
  Pallas kernels  115 us (96%)
  local copies, waits for them, and re-layouts  4.55 us (4%)
    pallas_call x1, Pallas kernels, per_device(): pl.pallas_call(kernel, out_shape=(jax.ShapeDtypeStruct((TOK, GROUP * HD),...  115 us
    unnamed x7, local copies, waits for them, and re-layouts  4.55 us

profile of v1, /device:TPU:0, one launch (start us, length us, event | category | flops | bytes accessed | tf_op | source)
XLA Modules:
  0.0 119.9 jit_solution(13091446252451033390)
XLA Ops:
  0.6 114.6 %attention_backward.1 = (bf16[1024,1024]{1,0:T(8,128)(2,1)}, bf16[1024,128]{1,0:T(8,128)(2,1)}, bf16[1024,128]{1,0:T(8,128)(2,1)}) custom-call(bf16[1024,1024]{1,0:T(8,128)(2,1)} %q_hbm.1, bf16[1024,128]{1,0:T(8,128)(2,1)} %k_hbm.1, bf16[1024,128]{1,0:T(8,128)(2,1)} %v_hbm.1, bf16[1024,1024]{1,0:T(8,128)(2,1)} %o_hbm.1, bf16[1024,640]{1,0:T(8,128)(2,1)} %og_hbm.1, ...), custom_call_target="tpu_custom_call" | custom-call | tf_op jit(solution)/shard_map/attention_backward/pallas_call | solution.py:274
  115.3 0.0 copy-start.1
  115.3 0.0 copy-start
  115.3 3.1 %copy.14 = bf16[1024,1024]{1,0:T(8,128)(2,1)} copy(bf16[1024,1024]{1,0:T(8,128)(2,1)} %get-tuple-element.6) | data formatting | bytes 4194304
  118.4 0.0 copy-done.1
  118.4 0.7 copy.15
  119.1 0.0 copy-done
  119.2 0.7 copy.16
Async XLA Ops:
  115.3 3.2 %copy-start.1 = (bf16[1024,128]{1,0:T(8,128)(2,1)S(1)}, bf16[1024,128]{1,0:T(8,128)(2,1)}, u32[]{:S(2)}) copy-start(bf16[1024,128]{1,0:T(8,128)(2,1)} %get-tuple-element.7) | copy-start | bytes 786436
  115.3 3.9 %copy-start = (bf16[1024,128]{1,0:T(8,128)(2,1)S(1)}, bf16[1024,128]{1,0:T(8,128)(2,1)}, u32[]{:S(2)}) copy-start(bf16[1024,128]{1,0:T(8,128)(2,1)} %get-tuple-element.8) | copy-start | bytes 786436

commit v2 on v1

v2 whole, which is shorter than its diff:
```python
import functools
import math

import jax
import jax.numpy as jnp
from jax import lax
from jax.experimental import pallas as pl
from jax.experimental.pallas import tpu as pltpu
from jax.sharding import PartitionSpec as P

MESH = pl.DeviceIdType.MESH
TOK = 1024
HALF = 512
HD = 128
GROUP = 8
COLS = 640
D = 5120
LEADS = (3, 3, 2, 5)
PARTS = ((0, 128), (128, 128), (256, 128), (384, 128), (768, 128), (896, 128), (640, 128), (512, 128))
CHUNKS = len(PARTS)
EDGE = 16
TILES = ((0, 256), (256, 256), (768, 256), (640, 128), (512, 128))
NEED = (1, 3, 5, 6, 7)
FIRST = 1
EDGED = 2
FLOWS = 10
LOG2E = math.log2(math.e)
NT = (((1,), (1,)), ((), ()))
NN = (((1,), (0,)), ((), ()))
FROWS = 256


def dot(a, b, dims):
    return lax.dot_general(a, b, dims, preferred_element_type=jnp.float32)


def kernel(
    q_hbm, k_hbm, v_hbm, o_hbm, og_hbm, w_hbm, lse_ref, doc_ref,
    dq_hbm, dk_ref, dv_ref,
    dq_ref, gt, gat, wv, qv, ov, ot, key, val, key_t, dk_acc, dv_acc, dk_in, dv_in, dk_out, dv_out, part, p_wide, p_slim, bias, doc_col, doc_row,
    send, recv, kv_send, kv_recv, back_send, back_recv, load, store,
):
    heads = lax.axis_index("heads")
    ctx = lax.axis_index("ctx")
    n_ctx = lax.axis_size("ctx")
    plane, x = heads // 4, heads % 4
    x_left, x_right, x_far = (x + 3) % 4, (x + 1) % 4, (x + 2) % 4
    other = 1 - plane
    right = {"heads": plane * 4 + x_right}
    left = {"heads": plane * 4 + x_left}
    across = {"heads": other * 4 + x}
    after = {"ctx": (ctx + 1) % n_ctx}
    before = {"ctx": (ctx + n_ctx - 1) % n_ctx}

    def cell(pl_, x_, row, rows):
        col = pl.multiple_of((pl_ * 4 + x_) * COLS, 128)
        return gat.at[pl.ds(row, rows), pl.ds(col, COLS)]

    def flow(f, j, received=False):
        r0, rows = PARTS[j]
        low, hr = rows - EDGE * (j < EDGED), rows // 2
        to = (right, left, across, right, left, right, left, across, across, across)[f]
        first, rows = (
            (r0, rows), (r0, rows), (r0, rows), (r0, hr), (r0 + hr, hr),
            (r0, low), (r0, low), (r0, rows), (r0 + low, EDGE), (r0 + low, EDGE),
        )[f]
        sent = (
            (plane, x), (plane, x), (plane, x), (plane, x_left), (plane, x_right),
            (other, x), (other, x), (plane, x_far), (plane, x_left), (plane, x_right),
        )[f]
        filled = (
            (plane, x_left), (plane, x_right), (other, x), (plane, x_far), (plane, x_far),
            (other, x_left), (other, x_right), (other, x_far), (other, x_left), (other, x_right),
        )[f]
        dst = cell(*(filled if received else sent), first, rows)
        src = og_hbm.at[pl.ds(first, rows), :] if f < 3 and not received else dst
        return pltpu.make_async_remote_copy(
            src_ref=src, dst_ref=dst, send_sem=send.at[f, j], recv_sem=recv.at[f, j],
            device_id=to, device_id_type=MESH,
        )

    def start(f, j):
        if f < 8 or j < EDGED:
            flow(f, j).start()

    def arrived(f, j):
        if f < 8 or j < EDGED:
            flow(f, j, received=True).wait_recv()

    def own(j):
        for f in range(3):
            start(f, j)

    def near(j):
        arrived(0, j)
        start(3, j)
        start(8, j)
        arrived(1, j)
        start(4, j)
        start(9, j)

    def crossed(j):
        arrived(2, j)
        start(5, j)
        start(6, j)

    def far(j):
        arrived(3, j)
        arrived(4, j)
        start(7, j)

    done = [0, 0, 0, 0]

    def advance(k, upto):
        while done[k] < min(upto + 1, CHUNKS):
            (near, crossed, far, own)[k](done[k])
            done[k] += 1

    def tick(t):
        for k in (0, 1, 3):
            advance(k, t + LEADS[k])

    def stage_c(j):
        if j < CHUNKS:
            for f in (5, 6, 8, 9, 7):
                arrived(f, j)

    def kv_copy(i, received=False):
        buf = (key, val)[i]
        src = (k_hbm, v_hbm)[i].at[pl.ds(HALF, HALF), :]
        dst = buf.at[pl.ds(0, HALF), :]
        return pltpu.make_async_remote_copy(
            src_ref=src, dst_ref=dst, send_sem=kv_send.at[i], recv_sem=kv_recv.at[i],
            device_id=after, device_id_type=MESH,
        )

    def back_copy(i):
        return pltpu.make_async_remote_copy(
            src_ref=(dk_out, dv_out)[i], dst_ref=(dk_in, dv_in)[i],
            send_sem=back_send.at[i], recv_sem=back_recv.at[i],
            device_id=before, device_id_type=MESH,
        )

    loads = [
        pltpu.make_async_copy(k_hbm, key.at[pl.ds(HALF, TOK), :], load.at[0]),
        pltpu.make_async_copy(v_hbm, val.at[pl.ds(HALF, TOK), :], load.at[1]),
        pltpu.make_async_copy(q_hbm, qv, load.at[2]),
        pltpu.make_async_copy(o_hbm, ov, load.at[3]),
        pltpu.make_async_copy(og_hbm, cell(plane, x, 0, TOK), load.at[4]),
        pltpu.make_async_copy(w_hbm, wv, load.at[5]),
    ]
    for c in loads:
        c.start()

    barrier = pltpu.get_barrier_semaphore()
    for d in (right, left, across, after, before):
        pl.semaphore_signal(barrier, inc=1, device_id=d, device_id_type=MESH)
    pl.semaphore_wait(barrier, 5)
    advance(3, LEADS[3] - 3)
    for i in range(2):
        kv_copy(i).start()

    dk_acc[...] = jnp.zeros_like(dk_acc)
    dv_acc[...] = jnp.zeros_like(dv_acc)
    half = ctx * 2
    n_half = n_ctx * 2
    for b in range(3):
        docs = doc_ref[(half + n_half - 1 + b) % n_half].astype(jnp.float32)
        doc_row[:, b * HALF:(b + 1) * HALF] = docs
        doc_col[b * HALF:(b + 1) * HALF, :] = jnp.broadcast_to(docs, (128, HALF)).T

    scale = 1.0 / math.sqrt(HD)

    def span(i):
        r0, n = TILES[i]
        return r0, n, r0 // HALF * HALF, HALF + r0 % HALF + n

    def set_bias(i):
        r0, n, k0, kk = span(i)
        row = doc_row[:, HALF + r0:HALF + r0 + n]
        for lo in range(0, kk, n):
            col = doc_col[k0 + lo:k0 + lo + n, :]
            same = (col if n == 128 else jnp.concatenate([col, col], axis=1)) == row
            if lo + n == kk:
                kp = lax.broadcasted_iota(jnp.int32, (n, n), 0)
                qp = lax.broadcasted_iota(jnp.int32, (n, n), 1)
                same = same & (kp <= qp)
            bias[lo:lo + n, :n] = jnp.where(same, 0.0, -1e30)

    def project(first, n, planes=None, start=True, end=True, at=0):
        def body(hp, carry):
            feats = pl.ds(pl.multiple_of(hp * 2 * HD, 2 * HD), 2 * HD)
            cols = slice(None) if planes is None else pl.ds(pl.multiple_of(planes * (D // 2), D // 2), D // 2)
            got = dot(wv[feats, cols], gat[first:first + n, cols], NT)
            if not start:
                got = part[feats, at:at + n] + got
            if end:
                gt[feats, :n] = got.astype(jnp.bfloat16)
            else:
                part[feats, :n] = got
            return carry

        lax.fori_loop(0, GROUP // 2, body, 0)

    def held(i, h):
        _, n, _, kk = span(i)
        base = GROUP * (0, 768, 1792, 0, 768)[i]
        rows = pl.ds(pl.multiple_of(base + h * kk, 128), kk)
        return (p_wide if n == 256 else p_slim).at[rows, :]

    def weigh(i):
        r0, n, k0, kk = span(i)
        set_bias(i)

        def head(h):
            q = qv[r0:r0 + n, pl.ds(pl.multiple_of(h * HD, HD), HD)]
            lo = r0 // 256 * 256
            lse = lse_ref[pl.ds(h, 1), lo:lo + 256][:, r0 - lo:r0 - lo + n] * LOG2E
            s = dot(key[k0:k0 + kk, :], q, NT)
            p = jnp.exp2((s * (scale * LOG2E) - lse) + bias[:kk, :n])
            held(i, h)[...] = p.astype(jnp.bfloat16)

        def body(hp, carry):
            head(hp * 2)
            head(hp * 2 + 1)
            return carry

        lax.fori_loop(0, GROUP // 2, body, 0)

    def attend(i, first, last):
        r0, n, k0, kk = span(i)

        def head(h):
            c0 = pl.multiple_of(h * HD, HD)
            g = gt[pl.ds(c0, HD), :n]
            q = qv[r0:r0 + n, pl.ds(c0, HD)]
            o = ot[pl.ds(c0, HD), r0:r0 + n]
            delta = jnp.sum(g.astype(jnp.float32) * o.astype(jnp.float32), axis=0, keepdims=True)
            p = held(i, h)[...]
            dp = dot(val[k0:k0 + kk, :], g, NN)
            ds = (p.astype(jnp.float32) * (dp - delta)).astype(jnp.bfloat16)
            dv_acc[k0:k0 + kk, :] += dot(p, g, NT)
            dk_acc[k0:k0 + kk, :] += dot(ds, q, NN)
            dq_t = dot(key_t[:, k0:k0 + kk], ds, NN) * scale
            dq_ref[r0:r0 + n, pl.ds(c0, HD)] = dq_t.T.astype(jnp.bfloat16)

        def body(hp, carry):
            head(hp * 2)
            head(hp * 2 + 1)
            return carry

        lax.fori_loop(first // 2, last // 2, body, 0)

    def out_copy(i):
        r0, n = TILES[i]
        return pltpu.make_async_copy(dq_ref.at[pl.ds(r0, n), :], dq_hbm.at[pl.ds(r0, n), :], store.at[i])

    def back():
        dk_out[...] = dk_acc[:HALF, :].astype(jnp.bfloat16)
        dv_out[...] = dv_acc[:HALF, :].astype(jnp.bfloat16)
        for b in range(2):
            back_copy(b).start()

    def store_rows(i):
        out_copy(i).start()

    for c in (loads[0], loads[1], loads[2]):
        c.wait()
    key_t[:, HALF:] = key[HALF:, :].T
    weigh(2)
    tick(-3)
    weigh(3)
    tick(-2)
    weigh(4)
    advance(2, LEADS[2] - 2)
    loads[3].wait()

    def turn(h, carry):
        c0 = pl.multiple_of(h * HD, HD)
        ot[pl.ds(c0, HD), :] = ov[:, pl.ds(c0, HD)].T
        return carry

    lax.fori_loop(0, GROUP, turn, 0)
    tick(-1)
    for i in range(2):
        kv_copy(i).wait_recv()
    key_t[:, :HALF] = key[:HALF, :].T
    weigh(0)
    advance(2, LEADS[2] - 1)
    weigh(1)
    loads[4].wait()
    loads[5].wait()

    windows = (
        [],
        [(project, 0, 256), (attend, 0, 0, 4)],
        [(attend, 0, 4, 8), (store_rows, 0)],
        [(project, 256, 256), (attend, 1, 0, 4)],
        [(attend, 1, 4, 8), (back,), (store_rows, 1)],
        [(project, 768, 256), (attend, 2, 0, 4), (attend, 2, 4, 8), (store_rows, 2),
         (project, 512, 256, plane, True, False)],
        [(project, 640, 128, other, False, True, 128), (attend, 3, 0, 8), (store_rows, 3)],
        [(project, 512, 128, other, False, True, 0), (attend, 4, 0, 8), (store_rows, 4)],
    )
    for j, work in enumerate(windows):
        stage_c(j)
        tick(j)
        for item in work[:FIRST]:
            item[0](*item[1:])
        advance(2, j + LEADS[2])
        for item in work[FIRST:]:
            item[0](*item[1:])

    for b in range(2):
        back_copy(b).wait()
        kv_copy(b).wait_send()

    for j in range(CHUNKS):
        for f in range(FLOWS):
            if f < 8 or j < EDGED:
                flow(f, j).wait_send()
    dk_ref[:HALF, :] = (dk_acc[HALF:TOK, :] * scale).astype(jnp.bfloat16)
    dk_ref[HALF:, :] = ((dk_acc[TOK:, :] + dk_in[...].astype(jnp.float32)) * scale).astype(jnp.bfloat16)
    dv_ref[:HALF, :] = dv_acc[HALF:TOK, :].astype(jnp.bfloat16)
    dv_ref[HALF:, :] = (dv_acc[TOK:, :] + dv_in[...].astype(jnp.float32)).astype(jnp.bfloat16)
    for i in range(len(TILES)):
        out_copy(i).wait()


def finish(dq, dk, dv, dq_out, dk_out, dv_out, dq_buf, dk_buf, dv_buf, sem_in, sem_out):
    pieces = [(dq.at[pl.ds(r, FROWS), :], dq_buf.at[pl.ds(r, FROWS), :], dq_out.at[pl.ds(r, FROWS), :]) for r in range(0, TOK, FROWS)]
    pieces += [(dk, dk_buf, dk_out), (dv, dv_buf, dv_out)]
    ins = [pltpu.make_async_copy(a, b, sem_in.at[i]) for i, (a, b, _) in enumerate(pieces)]
    outs = [pltpu.make_async_copy(b, c, sem_out.at[i]) for i, (_, b, c) in enumerate(pieces)]
    for c in ins:
        c.start()
    for a, b in zip(ins, outs):
        a.wait()
        b.start()
    for c in outs:
        c.wait()


def per_device(queries, keys, values, outputs, out_grad, out_weight, log_norm, doc_ids):
    bf, f32 = jnp.bfloat16, jnp.float32
    any_ = pl.BlockSpec(memory_space=pl.ANY)
    vm = pl.BlockSpec(memory_space=pltpu.VMEM)
    dma = pltpu.SemaphoreType.DMA
    wide = HALF + TOK
    shapes = (
        jax.ShapeDtypeStruct((TOK, GROUP * HD), bf),
        jax.ShapeDtypeStruct((TOK, HD), bf),
        jax.ShapeDtypeStruct((TOK, HD), bf),
    )
    grads = pl.pallas_call(
        kernel,
        out_shape=shapes,
        in_specs=[any_] * 6 + [vm] * 2,
        out_specs=(any_, vm, vm),
        scratch_shapes=[
            pltpu.VMEM((TOK, GROUP * HD), bf),
            pltpu.VMEM((GROUP * HD, 256), bf),
            pltpu.VMEM((TOK, D), bf),
            pltpu.VMEM((GROUP * HD, D), bf),
            pltpu.VMEM((TOK, GROUP * HD), bf),
            pltpu.VMEM((TOK, GROUP * HD), bf),
            pltpu.VMEM((GROUP * HD, TOK), bf),
            pltpu.VMEM((wide, HD), bf),
            pltpu.VMEM((wide, HD), bf),
            pltpu.VMEM((HD, wide), bf),
            pltpu.VMEM((wide, HD), f32),
            pltpu.VMEM((wide, HD), f32),
            pltpu.VMEM((HALF, HD), bf),
            pltpu.VMEM((HALF, HD), bf),
            pltpu.VMEM((HALF, HD), bf),
            pltpu.VMEM((HALF, HD), bf),
            pltpu.VMEM((GROUP * HD, 256), f32),
            pltpu.VMEM((GROUP * 2816, 256), bf),
            pltpu.VMEM((GROUP * 1408, 128), bf),
            pltpu.VMEM((TOK, 256), f32),
            pltpu.VMEM((wide, 128), f32),
            pltpu.VMEM((1, wide), f32),
            dma((FLOWS, CHUNKS)),
            dma((FLOWS, CHUNKS)),
            dma((2,)), dma((2,)), dma((2,)), dma((2,)), dma((6,)), dma((len(TILES),)),
        ],
        compiler_params=pltpu.CompilerParams(
            collective_id=0, has_side_effects=True, vmem_limit_bytes=58 * 2**20
        ),
        name="attention_backward",
    )(queries, keys, values, outputs, out_grad, out_weight, log_norm, doc_ids.reshape(32, 1, HALF))
    count = TOK // FROWS + 2
    return pl.pallas_call(
        finish, out_shape=shapes, in_specs=[any_] * 3, out_specs=(any_,) * 3, name="results",
        scratch_shapes=[pltpu.VMEM(a.shape, bf) for a in shapes] + [dma((count,)), dma((count,))],
    )(*grads)


def solution(mesh):
    in_specs = (
        P("ctx", "heads"), P("ctx", "heads"), P("ctx", "heads"), P("ctx", "heads"), P("ctx", "heads"),
        P("heads", None), P("heads", "ctx"), P(),
    )
    out_specs = (P("ctx", "heads"), P("ctx", "heads"), P("ctx", "heads"))
    return jax.shard_map(per_device, mesh=mesh, in_specs=in_specs, out_specs=out_specs, check_vma=False)
```

time: 120 us -> 98.5 us (0.82)
  Pallas kernels: 115 us -> 97.7 us
  local copies, waits for them, and re-layouts: 4.55 us -> 0 us
    pallas_call x1 -> x2, Pallas kernels: 115 us -> 97.7 us  [the longest x1 95.1 us: per_device(): pl.pallas_call(kernel, out_shape=shapes, in_specs=[any_] * 6 + [vm] * 2,...]
    unnamed x7 -> x0, local copies, waits for them, and re-layouts: 4.55 us -> none
where the time goes in v2:
time: 98.5 us; the launch traced here: 98.4 us
  Pallas kernels  97.7 us (99%)
    pallas_call x1, Pallas kernels, per_device(): pl.pallas_call(kernel, out_shape=shapes, in_specs=[any_] * 6 + [vm] * 2,...  95.1 us
    pallas_call x1, Pallas kernels, per_device(): pl.pallas_call(finish, out_shape=shapes, in_specs=[any_] * 3, out_specs=(...  2.63 us

profile of v2, /device:TPU:0, one launch (start us, length us, event | category | flops | bytes accessed | tf_op | source)
XLA Modules:
  0.0 98.4 jit_solution(3994133061027309213)
XLA Ops:
  0.6 95.1 %attention_backward.1 = (bf16[1024,1024]{1,0:T(8,128)(2,1)}, bf16[1024,128]{1,0:T(8,128)(2,1)}, bf16[1024,128]{1,0:T(8,128)(2,1)}) custom-call(bf16[1024,1024]{1,0:T(8,128)(2,1)} %q_hbm.1, bf16[1024,128]{1,0:T(8,128)(2,1)} %k_hbm.1, bf16[1024,128]{1,0:T(8,128)(2,1)} %v_hbm.1, bf16[1024,1024]{1,0:T(8,128)(2,1)} %o_hbm.1, bf16[1024,640]{1,0:T(8,128)(2,1)} %og_hbm.1, ...), custom_call_target="tpu_custom_call" | custom-call | tf_op jit(solution)/shard_map/attention_backward/pallas_call | solution.py:355
  95.7 2.6 %results.1 = (bf16[1024,1024]{1,0:T(8,128)(2,1)}, bf16[1024,128]{1,0:T(8,128)(2,1)}, bf16[1024,128]{1,0:T(8,128)(2,1)}) custom-call(bf16[1024,1024]{1,0:T(8,128)(2,1)} %get-tuple-element.6.dq, bf16[1024,128]{1,0:T(8,128)(2,1)} %get-tuple-element.7.dk, bf16[1024,128]{1,0:T(8,128)(2,1)} %get-tuple-element.8.dv), custom_call_target="tpu_custom_call" | custom-call | tf_op jit(solution)/shard_map/results/pallas_call | solution.py:393

commit v3 on v2

--- a/solution.py
+++ b/solution.py
@@ -16,13 +16,14 @@
 COLS = 640
 D = 5120
 LEADS = (3, 3, 2, 5)
-PARTS = ((0, 128), (128, 128), (256, 128), (384, 128), (768, 128), (896, 128), (640, 128), (512, 128))
+STARTS = (0, 128, 256, 384, 768, 896, 640, 512)
+SIZE = 128
+EDGE = 16
+TILES = ((0, 256), (256, 256), (768, 256), (512, 256))
+FINE = 128 // SIZE
+PARTS = tuple((r + k * SIZE, SIZE) for r in STARTS for k in range(FINE))
 CHUNKS = len(PARTS)
-EDGE = 16
-TILES = ((0, 256), (256, 256), (768, 256), (640, 128), (512, 128))
-NEED = (1, 3, 5, 6, 7)
-FIRST = 1
-EDGED = 2
+EDGED = 6
 FLOWS = 10
 LOG2E = math.log2(math.e)
 NT = (((1,), (1,)), ((), ()))
@@ -37,7 +38,7 @@
 def kernel(
     q_hbm, k_hbm, v_hbm, o_hbm, og_hbm, w_hbm, lse_ref, doc_ref,
     dq_hbm, dk_ref, dv_ref,
-    dq_ref, gt, gat, wv, qv, ov, ot, key, val, key_t, dk_acc, dv_acc, dk_in, dv_in, dk_out, dv_out, part, p_wide, p_slim, bias, doc_col, doc_row,
+    dq_ref, gt, gat, wv, qv, ov, ot, key, val, key_t, dk_acc, dv_acc, dk_in, dv_in, dk_out, dv_out, part, held, bias, doc_col, doc_row,
     send, recv, kv_send, kv_recv, back_send, back_recv, load, store,
 ):
     heads = lax.axis_index("heads")
@@ -180,33 +181,34 @@
         row = doc_row[:, HALF + r0:HALF + r0 + n]
         for lo in range(0, kk, n):
             col = doc_col[k0 + lo:k0 + lo + n, :]
-            same = (col if n == 128 else jnp.concatenate([col, col], axis=1)) == row
+            same = jnp.concatenate([col, col], axis=1) == row
             if lo + n == kk:
                 kp = lax.broadcasted_iota(jnp.int32, (n, n), 0)
                 qp = lax.broadcasted_iota(jnp.int32, (n, n), 1)
                 same = same & (kp <= qp)
-            bias[lo:lo + n, :n] = jnp.where(same, 0.0, -1e30)
-
-    def project(first, n, planes=None, start=True, end=True, at=0):
+            bias[lo:lo + n, :] = jnp.where(same, 0.0, -1e30)
+
+    def project(i, planes=None):
+        r0, n, _, _ = span(i)
+
         def body(hp, carry):
             feats = pl.ds(pl.multiple_of(hp * 2 * HD, 2 * HD), 2 * HD)
             cols = slice(None) if planes is None else pl.ds(pl.multiple_of(planes * (D // 2), D // 2), D // 2)
-            got = dot(wv[feats, cols], gat[first:first + n, cols], NT)
-            if not start:
-                got = part[feats, at:at + n] + got
-            if end:
-                gt[feats, :n] = got.astype(jnp.bfloat16)
+            got = dot(wv[feats, cols], gat[r0:r0 + n, cols], NT)
+            if planes is plane:
+                part[feats, :] = got
             else:
-                part[feats, :n] = got
+                if planes is other:
+                    got = part[feats, :] + got
+                gt[feats, :] = got.astype(jnp.bfloat16)
             return carry
 
         lax.fori_loop(0, GROUP // 2, body, 0)
 
-    def held(i, h):
-        _, n, _, kk = span(i)
-        base = GROUP * (0, 768, 1792, 0, 768)[i]
-        rows = pl.ds(pl.multiple_of(base + h * kk, 128), kk)
-        return (p_wide if n == 256 else p_slim).at[rows, :]
+    def kept(i, h):
+        kk = span(i)[3]
+        base = GROUP * (0, 768, 1792, 2816)[i]
+        return held.at[pl.ds(pl.multiple_of(base + h * kk, 256), kk), :]
 
     def weigh(i):
         r0, n, k0, kk = span(i)
@@ -214,11 +216,10 @@
 
         def head(h):
             q = qv[r0:r0 + n, pl.ds(pl.multiple_of(h * HD, HD), HD)]
-            lo = r0 // 256 * 256
-            lse = lse_ref[pl.ds(h, 1), lo:lo + 256][:, r0 - lo:r0 - lo + n] * LOG2E
+            lse = lse_ref[pl.ds(h, 1), r0:r0 + n] * LOG2E
             s = dot(key[k0:k0 + kk, :], q, NT)
-            p = jnp.exp2((s * (scale * LOG2E) - lse) + bias[:kk, :n])
-            held(i, h)[...] = p.astype(jnp.bfloat16)
+            p = jnp.exp2((s * (scale * LOG2E) - lse) + bias[:kk, :])
+            kept(i, h)[...] = p.astype(jnp.bfloat16)
 
         def body(hp, carry):
             head(hp * 2)
@@ -232,11 +233,11 @@
 
         def head(h):
             c0 = pl.multiple_of(h * HD, HD)
-            g = gt[pl.ds(c0, HD), :n]
+            g = gt[pl.ds(c0, HD), :]
             q = qv[r0:r0 + n, pl.ds(c0, HD)]
             o = ot[pl.ds(c0, HD), r0:r0 + n]
             delta = jnp.sum(g.astype(jnp.float32) * o.astype(jnp.float32), axis=0, keepdims=True)
-            p = held(i, h)[...]
+            p = kept(i, h)[...]
             dp = dot(val[k0:k0 + kk, :], g, NN)
             ds = (p.astype(jnp.float32) * (dp - delta)).astype(jnp.bfloat16)
             dv_acc[k0:k0 + kk, :] += dot(p, g, NT)
@@ -271,7 +272,6 @@
     tick(-3)
     weigh(3)
     tick(-2)
-    weigh(4)
     advance(2, LEADS[2] - 2)
     loads[3].wait()
 
@@ -291,24 +291,22 @@
     loads[4].wait()
     loads[5].wait()
 
-    windows = (
-        [],
-        [(project, 0, 256), (attend, 0, 0, 4)],
-        [(attend, 0, 4, 8), (store_rows, 0)],
-        [(project, 256, 256), (attend, 1, 0, 4)],
-        [(attend, 1, 4, 8), (back,), (store_rows, 1)],
-        [(project, 768, 256), (attend, 2, 0, 4), (attend, 2, 4, 8), (store_rows, 2),
-         (project, 512, 256, plane, True, False)],
-        [(project, 640, 128, other, False, True, 128), (attend, 3, 0, 8), (store_rows, 3)],
-        [(project, 512, 128, other, False, True, 0), (attend, 4, 0, 8), (store_rows, 4)],
-    )
-    for j, work in enumerate(windows):
+    windows = {
+        1: [(project, 0), (attend, 0, 0, 4)],
+        2: [(attend, 0, 4, 8), (store_rows, 0)],
+        3: [(project, 1), (attend, 1, 0, 4)],
+        4: [(attend, 1, 4, 8), (back,), (store_rows, 1)],
+        5: [(project, 2), (attend, 2, 0, 4), (attend, 2, 4, 8), (store_rows, 2), (project, 3, plane)],
+        7: [(project, 3, other), (attend, 3, 0, 8), (store_rows, 3)],
+    }
+    for j in range(CHUNKS):
         stage_c(j)
         tick(j)
-        for item in work[:FIRST]:
+        work = windows.get((j + 1) // FINE - 1, []) if (j + 1) % FINE == 0 else []
+        for item in work[:1]:
             item[0](*item[1:])
         advance(2, j + LEADS[2])
-        for item in work[FIRST:]:
+        for item in work[1:]:
             item[0](*item[1:])
 
     for b in range(2):
@@ -375,8 +373,7 @@
             pltpu.VMEM((HALF, HD), bf),
             pltpu.VMEM((HALF, HD), bf),
             pltpu.VMEM((GROUP * HD, 256), f32),
-            pltpu.VMEM((GROUP * 2816, 256), bf),
-            pltpu.VMEM((GROUP * 1408, 128), bf),
+            pltpu.VMEM((GROUP * 3584, 256), bf),
             pltpu.VMEM((TOK, 256), f32),
             pltpu.VMEM((wide, 128), f32),
             pltpu.VMEM((1, wide), f32),

time: 98.5 us -> 93.4 us (0.948)
  Pallas kernels: 97.7 us -> 92.3 us
    pallas_call x1, Pallas kernels: 95.1 us -> 89.7 us  [per_device(): pl.pallas_call(kernel, out_shape=shapes, in_specs=[any_] * 6 + [vm] * 2,...]
where the time goes in v3:
time: 93.4 us; the launch traced here: 92.9 us
  Pallas kernels  92.3 us (99%)
    pallas_call x1, Pallas kernels, per_device(): pl.pallas_call(kernel, out_shape=shapes, in_specs=[any_] * 6 + [vm] * 2,...  89.7 us
    pallas_call x1, Pallas kernels, per_device(): pl.pallas_call(finish, out_shape=shapes, in_specs=[any_] * 3, out_specs=(...  2.63 us

profile of v3, /device:TPU:0, one launch (start us, length us, event | category | flops | bytes accessed | tf_op | source)
XLA Modules:
  0.0 92.9 jit_solution(11504024063177933573)
XLA Ops:
  0.6 89.7 %attention_backward.1 = (bf16[1024,1024]{1,0:T(8,128)(2,1)}, bf16[1024,128]{1,0:T(8,128)(2,1)}, bf16[1024,128]{1,0:T(8,128)(2,1)}) custom-call(bf16[1024,1024]{1,0:T(8,128)(2,1)} %q_hbm.1, bf16[1024,128]{1,0:T(8,128)(2,1)} %k_hbm.1, bf16[1024,128]{1,0:T(8,128)(2,1)} %v_hbm.1, bf16[1024,1024]{1,0:T(8,128)(2,1)} %o_hbm.1, bf16[1024,640]{1,0:T(8,128)(2,1)} %og_hbm.1, ...), custom_call_target="tpu_custom_call" | custom-call | tf_op jit(solution)/shard_map/attention_backward/pallas_call | solution.py:353
  90.3 2.6 %results.1 = (bf16[1024,1024]{1,0:T(8,128)(2,1)}, bf16[1024,128]{1,0:T(8,128)(2,1)}, bf16[1024,128]{1,0:T(8,128)(2,1)}) custom-call(bf16[1024,1024]{1,0:T(8,128)(2,1)} %get-tuple-element.6.dq, bf16[1024,128]{1,0:T(8,128)(2,1)} %get-tuple-element.7.dk, bf16[1024,128]{1,0:T(8,128)(2,1)} %get-tuple-element.8.dv), custom_call_target="tpu_custom_call" | custom-call | tf_op jit(solution)/shard_map/results/pallas_call | solution.py:390

commit v4 on v3

--- a/solution.py
+++ b/solution.py
@@ -303,10 +303,11 @@
         stage_c(j)
         tick(j)
         work = windows.get((j + 1) // FINE - 1, []) if (j + 1) % FINE == 0 else []
-        for item in work[:1]:
+        ahead = 3 if j == 5 else 1
+        for item in work[:ahead]:
             item[0](*item[1:])
         advance(2, j + LEADS[2])
-        for item in work[1:]:
+        for item in work[ahead:]:
             item[0](*item[1:])
 
     for b in range(2):

time: 93.4 us -> 96.7 us (1.035)
  Pallas kernels: 92.3 us -> 95.9 us
    pallas_call x1, Pallas kernels: 89.7 us -> 93.3 us  [per_device(): pl.pallas_call(kernel, out_shape=shapes, in_specs=[any_] * 6 + [vm] * 2,...]
where the time goes in v4:
time: 96.7 us; the launch traced here: 96.5 us
  Pallas kernels  95.9 us (99%)
    pallas_call x1, Pallas kernels, per_device(): pl.pallas_call(kernel, out_shape=shapes, in_specs=[any_] * 6 + [vm] * 2,...  93.3 us
    pallas_call x1, Pallas kernels, per_device(): pl.pallas_call(finish, out_shape=shapes, in_specs=[any_] * 3, out_specs=(...  2.63 us

profile of v4, /device:TPU:0, one launch (start us, length us, event | category | flops | bytes accessed | tf_op | source)
XLA Modules:
  0.0 96.5 jit_solution(372293951096186885)
XLA Ops:
  0.6 93.3 %attention_backward.1 = (bf16[1024,1024]{1,0:T(8,128)(2,1)}, bf16[1024,128]{1,0:T(8,128)(2,1)}, bf16[1024,128]{1,0:T(8,128)(2,1)}) custom-call(bf16[1024,1024]{1,0:T(8,128)(2,1)} %q_hbm.1, bf16[1024,128]{1,0:T(8,128)(2,1)} %k_hbm.1, bf16[1024,128]{1,0:T(8,128)(2,1)} %v_hbm.1, bf16[1024,1024]{1,0:T(8,128)(2,1)} %o_hbm.1, bf16[1024,640]{1,0:T(8,128)(2,1)} %og_hbm.1, ...), custom_call_target="tpu_custom_call" | custom-call | tf_op jit(solution)/shard_map/attention_backward/pallas_call | solution.py:354
  93.9 2.6 %results.1 = (bf16[1024,1024]{1,0:T(8,128)(2,1)}, bf16[1024,128]{1,0:T(8,128)(2,1)}, bf16[1024,128]{1,0:T(8,128)(2,1)}) custom-call(bf16[1024,1024]{1,0:T(8,128)(2,1)} %get-tuple-element.6.dq, bf16[1024,128]{1,0:T(8,128)(2,1)} %get-tuple-element.7.dk, bf16[1024,128]{1,0:T(8,128)(2,1)} %get-tuple-element.8.dv), custom_call_target="tpu_custom_call" | custom-call | tf_op jit(solution)/shard_map/results/pallas_call | solution.py:391
